TPU v7x, 32 devices: a whole 2x2x4 slice. The times are simulated.
32 devices in a mesh: wa: 2 (over core), ha: 16 (over z, y, x).
Axes of the slice: x: 2, y: 2, z: 4, core: 2. Of those that a mesh axis runs over, the one named last changes fastest.
Arguments:
- tokens: bfloat16 [256, 16384], P('ha', 'wa'), may hold values from -6 to 6
- cotangent: bfloat16 [256, 16384], P('ha', 'wa'), may hold values from -6 to 6
- gate_weight: bfloat16 [16384, 12288], P('wa', 'ha'), may hold values from -0.046875 to 0.046875
- up_weight: bfloat16 [16384, 12288], P('wa', 'ha'), may hold values from -0.046875 to 0.046875
- down_weight: bfloat16 [12288, 16384], P('ha', 'wa'), may hold values from -0.0546875 to 0.0546875
Outputs:
- input_grad: bfloat16 [256, 16384], P('ha', 'wa')
- gate_weight_grad: bfloat16 [16384, 12288], P('wa', 'ha')
- up_weight_grad: bfloat16 [16384, 12288], P('wa', 'ha')
- down_weight_grad: bfloat16 [12288, 16384], P('ha', 'wa')
All inputs are finite; a program needn't handle non-finite values.
Results may differ from a plain program's by a relative error of at most 0.0049.
Values may be sent and summed in bfloat16 or wider, within the bound.
A program may use at most 192 MiB of HBM per device.

v0:
```python
import jax
import jax.numpy as jnp
from jax import lax
from jax.sharding import PartitionSpec as P

TOKENS = 256


def pointwise(gate_sum, up_sum, hidden_grad):
    sigma = jax.nn.sigmoid(gate_sum)
    hidden = (gate_sum * sigma * up_sum).astype(jnp.bfloat16)
    gate_grad = (hidden_grad * up_sum * sigma * (1.0 + gate_sum * (1.0 - sigma))).astype(
        jnp.bfloat16
    )
    up_grad = (hidden_grad * gate_sum * sigma).astype(jnp.bfloat16)
    return (hidden, gate_grad, up_grad)


def contract_rows(left, right):
    return lax.dot_general(
        left, right, (((0,), (0,)), ((), ())), preferred_element_type=jnp.float32
    )


def contract_cols(left, right):
    return lax.dot_general(
        left, right, (((1,), (1,)), ((), ())), preferred_element_type=jnp.float32
    )


def on_device(tokens, cotangent, gate_weight, up_weight, down_weight):
    factor = TOKENS ** (-0.5)
    inputs_all = lax.all_gather(tokens, "ha", axis=0, tiled=True)
    grads_all = lax.all_gather(cotangent, "ha", axis=0, tiled=True)
    gate_part = jnp.dot(inputs_all, gate_weight, preferred_element_type=jnp.float32)
    up_part = jnp.dot(inputs_all, up_weight, preferred_element_type=jnp.float32)
    hidden_part = contract_cols(grads_all, down_weight)
    gate_sum, up_sum, hidden_grad = lax.psum((gate_part, up_part, hidden_part), "wa")
    hidden, gate_grad, up_grad = pointwise(gate_sum, up_sum, hidden_grad)
    down_weight_grad = (contract_rows(hidden, grads_all) * factor).astype(jnp.bfloat16)
    gate_weight_grad = (contract_rows(inputs_all, gate_grad) * factor).astype(jnp.bfloat16)
    up_weight_grad = (contract_rows(inputs_all, up_grad) * factor).astype(jnp.bfloat16)
    input_grad = lax.psum_scatter(
        contract_cols(gate_grad, gate_weight) + contract_cols(up_grad, up_weight),
        "ha",
        scatter_dimension=0,
        tiled=True,
    )
    return (input_grad.astype(jnp.bfloat16), gate_weight_grad, up_weight_grad, down_weight_grad)


def solution(mesh):
    placed = (P("ha", "wa"), P("ha", "wa"), P("wa", "ha"), P("wa", "ha"), P("ha", "wa"))
    return jax.shard_map(
        on_device,
        mesh=mesh,
        in_specs=placed,
        out_specs=(P("ha", "wa"), P("wa", "ha"), P("wa", "ha"), P("ha", "wa")),
        check_vma=False,
    )
```

profile of v0, /device:TPU:0, one launch (start us, length us, event | category | flops | bytes accessed | tf_op | source)
XLA Modules:
  0.0 417.8 jit_solution(18433757458981397295)
XLA Ops:
  7.2 0.0 all-gather.5.cloned.1.call-start
  7.2 0.7 all-gather.5.cloned.1.call-update
  7.9 0.0 all-gather.3.cloned.1.call-start
  7.9 0.7 all-gather.3.cloned.1.call-update
  8.6 0.0 all-reduce.3.cloned.1.call-start
  8.7 80.9 %all-gather.5.cloned.1.call-done = bf16[256,8192]{1,0:T(8,128)(2,1)} async-done(((bf16[16,8192]{1,0:T(8,128)(2,1)}), bf16[256,8192]{1,0:T(8,128)(2,1)}) %all-gather.5.cloned.1.call-update) | async-done | bytes 4194320 | tf_op jit(solution)/shard_map/all_gather | solution.py:33
  89.6 0.0 copy-start.2
  89.6 10.3 %fusion.6 = f32[256,768]{1,0:T(8,128)} fusion(bf16[256,8192]{1,0:T(8,128)(2,1)} %all-gather.5.cloned.1.call-done, bf16[8192,768]{1,0:T(8,128)(2,1)} %param.7), kind=kOutput, calls=%fused_computation.14 | convolution fusion | flops 3221225472 | bytes 17563648 | tf_op jit(solution)/shard_map/dot_general | solution.py:35
  99.9 0.0 copy-done.2
  99.9 7.3 %fusion.5 = f32[256,768]{1,0:T(8,128)} fusion(bf16[256,8192]{1,0:T(8,128)(2,1)S(1)} %copy-done.2, bf16[8192,768]{1,0:T(8,128)(2,1)} %param.8), kind=kOutput, calls=%fused_computation.13 | convolution fusion | flops 3221225472 | bytes 17563648 | tf_op jit(solution)/shard_map/dot_general | solution.py:36
  107.2 59.5 %all-gather.3.cloned.1.call-done = bf16[256,8192]{1,0:T(8,128)(2,1)} async-done(((bf16[16,8192]{1,0:T(8,128)(2,1)}), bf16[256,8192]{1,0:T(8,128)(2,1)}) %all-gather.3.cloned.1.call-update) | async-done | bytes 4194320 | tf_op jit(solution)/shard_map/all_gather | solution.py:34
  166.7 10.2 %fusion.4 = f32[256,768]{1,0:T(8,128)} fusion(bf16[256,8192]{1,0:T(8,128)(2,1)} %all-gather.3.cloned.1.call-done, bf16[768,8192]{1,0:T(8,128)(2,1)} %param.9), kind=kOutput, calls=%fused_computation.12 | convolution fusion | flops 3221225472 | bytes 17563648 | tf_op jit(solution)/shard_map/dot_general | solution.py:26
  176.9 0.0 all-reduce.3.cloned.1.call-update
  176.9 0.2 reduce-scatter.2.cloned.1.call-start
  177.1 20.3 %all-reduce.3.cloned.1.call-done = (f32[256,768]{1,0:T(8,128)}, f32[256,768]{1,0:T(8,128)}, f32[256,768]{1,0:T(8,128)}) async-done(((f32[256,768]{1,0:T(8,128)}, f32[256,768]{1,0:T(8,128)}, f32[256,768]{1,0:T(8,128)}), (f32[256,768]{1,0:T(8,128)}, f32[256,768]{1,0:T(8,128)}, f32[256,768]{1,0:T(8,128)})) %all-reduce.3.cloned.1.call-update) | async-done | bytes 2359312 | tf_op jit(solution)/shard_map/psum | solution.py:38
  197.5 2.0 multiply_convert_fusion.4
  199.5 14.7 %fusion.7 = f32[256,8192]{1,0:T(8,128)} fusion(bf16[256,768]{1,0:T(8,128)(2,1)S(1)} %get-tuple-element.12, bf16[8192,768]{1,0:T(8,128)(2,1)} %param.7), kind=kOutput, calls=%fused_computation.15 | convolution fusion | flops 3221225472 | bytes 21364736 | tf_op jit(solution)/shard_map/dot_general | solution.py:26
  214.2 16.1 %convolution_add_fusion = f32[256,8192]{1,0:T(8,128)} fusion(f32[256,8192]{1,0:T(8,128)} %fusion.7, bf16[256,768]{1,0:T(8,128)(2,1)S(1)} %get-tuple-element.11, bf16[8192,768]{1,0:T(8,128)(2,1)} %param.8), kind=kOutput, calls=%fused_computation.5 | convolution fusion | flops 3223322624 | bytes 29753344 | tf_op jit(solution)/shard_map/dot_general | solution.py:26
  230.3 0.0 reduce-scatter.2.cloned.1.call-update
  230.3 8.8 %fusion = bf16[8192,768]{0,1:T(8,128)(2,1)} fusion(bf16[256,768]{1,0:T(8,128)(2,1)S(1)} %get-tuple-element.12, bf16[256,8192]{1,0:T(8,128)(2,1)} %all-gather.5.cloned.1.call-done), kind=kOutput, calls=%fused_computation.3 | convolution fusion | flops 3233808384 | bytes 17170432 | tf_op jit(solution)/shard_map/dot_general | solution.py:20
  239.1 16.6 %copy.9 = bf16[8192,768]{1,0:T(8,128)(2,1)} copy(bf16[8192,768]{0,1:T(8,128)(2,1)} %fusion) | data formatting | bytes 25165824
  255.7 8.9 %fusion.1 = bf16[8192,768]{0,1:T(8,128)(2,1)} fusion(bf16[256,768]{1,0:T(8,128)(2,1)S(1)} %get-tuple-element.11, bf16[256,8192]{1,0:T(8,128)(2,1)} %all-gather.5.cloned.1.call-done), kind=kOutput, calls=%fused_computation.4 | convolution fusion | flops 3233808384 | bytes 17170432 | tf_op jit(solution)/shard_map/dot_general | solution.py:20
  264.6 0.0 copy-start
  264.6 0.0 copy-start.1
  264.6 16.7 %copy.10 = bf16[8192,768]{1,0:T(8,128)(2,1)} copy(bf16[8192,768]{0,1:T(8,128)(2,1)} %fusion.1) | data formatting | bytes 25165824
  281.3 0.0 copy-done
  281.3 0.0 copy-done.1
  281.3 8.9 %multiply_convert_fusion = bf16[768,8192]{1,0:T(8,128)(2,1)} fusion(bf16[256,8192]{1,0:T(8,128)(2,1)} %all-gather.3.cloned.1.call-done, f32[256,768]{1,0:T(8,128)S(1)} %copy-done.1, f32[256,768]{1,0:T(8,128)S(1)} %copy-done), kind=kOutput, calls=%fused_computation | convolution fusion | flops 3234988032 | bytes 18350080 | tf_op jit(solution)/shard_map/dot_general | solution.py:20
  290.2 119.3 %reduce-scatter.2.cloned.1.call-done = f32[16,8192]{1,0:T(8,128)} async-done(((f32[256,8192]{1,0:T(8,128)}), f32[16,8192]{1,0:T(8,128)}) %reduce-scatter.2.cloned.1.call-update) | async-done | bytes 524304 | tf_op jit(solution)/shard_map/reduce_scatter | solution.py:43
  409.5 1.8 convert_element_type.29
Async XLA Ops:
  7.2 82.4 %all-gather.5.cloned.1.call-start = ((), (), s32[]{:S(2)}) async-start(), calls=%async_computation.2 | async-start | bytes 4456448 | tf_op jit(solution)/shard_map/all_gather | solution.py:33
  7.9 158.8 %all-gather.3.cloned.1.call-start = ((), (), s32[]{:S(2)}) async-start(), calls=%async_computation.1 | async-start | bytes 4456448 | tf_op jit(solution)/shard_map/all_gather | solution.py:34
  8.6 188.8 %all-reduce.3.cloned.1.call-start = ((), (), s32[]{:S(2)}) async-start(), calls=%async_computation.4 | async-start | bytes 4718592 | tf_op jit(solution)/shard_map/psum | solution.py:38
  89.6 10.3 %copy-start.2 = (bf16[256,8192]{1,0:T(8,128)(2,1)S(1)}, bf16[256,8192]{1,0:T(8,128)(2,1)}, u32[]{:S(2)}) copy-start(bf16[256,8192]{1,0:T(8,128)(2,1)} %all-gather.5.cloned.1.call-done) | copy-start | bytes 12582916
  176.9 232.6 %reduce-scatter.2.cloned.1.call-start = ((), (), s32[]{:S(2)}) async-start(), calls=%async_computation.3 | async-start | bytes 8912896 | tf_op jit(solution)/shard_map/reduce_scatter | solution.py:43
  264.6 16.7 %copy-start = (f32[256,768]{1,0:T(8,128)S(1)}, f32[256,768]{1,0:T(8,128)}, u32[]{:S(2)}) copy-start(f32[256,768]{1,0:T(8,128)} %get-tuple-element.8) | copy-start | bytes 2359300
  264.6 16.7 %copy-start.1 = (f32[256,768]{1,0:T(8,128)S(1)}, f32[256,768]{1,0:T(8,128)}, u32[]{:S(2)}) copy-start(f32[256,768]{1,0:T(8,128)} %get-tuple-element.10) | copy-start | bytes 2359300
Sparse Core Ops, SparseCore 0:
  10.8 78.7 all-gather.4
  92.3 74.3 all-gather.2
  177.0 20.3 all-reduce.2
  230.4 179.0 reduce-scatter.1
where the time goes:
time: 420 us; the launch traced here: 418 us
  waiting for transfers between devices  281 us (67%)
  matrix products  85.2 us (20%)
  local copies, waits for them, and re-layouts  33.4 us (8%)
  between operations  13.8 us (3%)
    reduce_scatter x1, waiting for transfers between devices, on_device(): lax.psum_scatter(contract_cols(gate_grad, gate_weight) + contract_cols(up...  119 us
    all_gather x1, waiting for transfers between devices, on_device(): inputs_all = lax.all_gather(tokens, 'ha', axis=0, tiled=True)  80.9 us
    all_gather x1, waiting for transfers between devices, on_device(): grads_all = lax.all_gather(cotangent, 'ha', axis=0, tiled=True)  59.5 us
    dot_general x3, matrix products, contract_cols(): lax.dot_general(left, right, (((1,), (1,)), ((), ())), preferred_element_...  41 us
    unnamed x8, local copies, waits for them, and re-layouts  33.4 us
    dot_general x3, matrix products, contract_rows(): lax.dot_general(left, right, (((0,), (0,)), ((), ())), preferred_element_...  26.6 us
    psum x1, waiting for transfers between devices, on_device(): lax.psum((gate_part, up_part, hidden_part), 'wa')  20.3 us
    dot_general x1, matrix products, on_device(): jnp.dot(inputs_all, gate_weight, preferred_element_type=jnp.float32)  10.3 us
  transfers between devices with their start and end apart: 4, of which 4 were waited for; matrix products, arithmetic and copies ran while one was open for 19% of the time, Pallas kernels for 0%

commit v1 on v0

v1 whole, which is shorter than its diff:
```python
import functools
import itertools

import jax
import jax.numpy as jnp
from jax import lax
from jax.experimental import pallas as pl
from jax.experimental.pallas import tpu as pltpu
from jax.sharding import PartitionSpec as P

MESH = pl.DeviceIdType.MESH
BF16, F32 = jnp.bfloat16, jnp.float32
VMEM_LIMIT = 60 * 1024 * 1024

GATHER_PARTS = ((0, 7, (0, 1, 2)), (7, 7, (0, 2, 1)), (14, 1, (2, 1, 0)), (15, 1, (1, 2, 0)))
SUM_PARTS = (
    (0, 4, (2, 1, 0)),
    (7, 4, (1, 2, 0)),
    (14, 1, (0, 1, 2)),
    (15, 1, (0, 2, 1)),
    (4, 3, (2, 1, 0)),
    (11, 3, (1, 2, 0)),
)


def pointwise(gate_sum, up_sum, hidden_grad):
    sigma = jax.nn.sigmoid(gate_sum)
    hidden = (gate_sum * sigma * up_sum).astype(BF16)
    gate_grad = (hidden_grad * up_sum * sigma * (1.0 + gate_sum * (1.0 - sigma))).astype(BF16)
    up_grad = (hidden_grad * gate_sum * sigma).astype(BF16)
    return (hidden, gate_grad, up_grad)


def contract_rows(left, right):
    return lax.dot_general(left, right, (((0,), (0,)), ((), ())), preferred_element_type=F32)


def contract_cols(left, right):
    return lax.dot_general(left, right, (((1,), (1,)), ((), ())), preferred_element_type=F32)


def main_kernel(
    dims, cores,
    tok_ref, cot_ref, wg_ref, wu_ref, wd_ref,
    xall_ref, gall_ref, hidden_ref, gg_ref, ug_ref, out_ref,
    x_buf, g_buf, wg, wu, wd, part, wa_recv, rs_recv,
    in_sem, w_sem, copy_sem, ag_send, ag_recv, wa_send, wa_recv_sem, rs_send, rs_sem,
):
    rows, width = tok_ref.shape
    ff = wg_ref.shape[1]
    tokens = rows * dims[0] * dims[1] * dims[2]
    unit = width // 16
    ha = lax.axis_index("ha")
    core = lax.axis_index("wa")
    me = (
        lax.div(ha, dims[1] * dims[2]),
        lax.rem(lax.div(ha, dims[2]), dims[1]),
        lax.rem(ha, dims[2]),
    )

    def moved(at, axis, by):
        pos = list(at)
        pos[axis] = lax.rem(at[axis] + by + dims[axis], dims[axis])
        return tuple(pos)

    def index(at):
        return (at[0] * dims[1] + at[1]) * dims[2] + at[2]

    def origin(kid):
        return tuple(lax.rem(me[a] - kid[a] + dims[a], dims[a]) for a in range(3))

    barrier = pltpu.get_barrier_semaphore()
    greeted = 0
    for axis in range(3):
        for by in range(1, dims[axis]):
            pl.semaphore_signal(
                barrier, inc=1, device_id={"ha": index(moved(me, axis, by))}, device_id_type=MESH
            )
            greeted += 1
    for by in range(1, cores):
        pl.semaphore_signal(
            barrier, inc=1, device_id={"wa": lax.rem(core + by, cores)}, device_id_type=MESH
        )
        greeted += 1

    bufs = (x_buf, g_buf)
    own = [
        pltpu.make_async_copy(ref, buf.at[me[0], me[1], me[2]], in_sem.at[i])
        for i, (ref, buf) in enumerate(((tok_ref, x_buf), (cot_ref, g_buf)))
    ]
    for copy in own:
        copy.start()
    loads = [
        pltpu.make_async_copy(ref, buf, w_sem.at[i])
        for i, (ref, buf) in enumerate(((wg_ref, wg), (wu_ref, wu), (wd_ref, wd)))
    ]
    pl.semaphore_wait(barrier, greeted)

    def sem_id(arr, p, kid):
        return ((arr * len(GATHER_PARTS) + p) * dims[0] + kid[0]) * dims[1] * dims[2] + (
            kid[1] * dims[2] + kid[2]
        )

    sends = {0: [], 1: []}

    def shard(arr, p, kid):
        start, size, _ = GATHER_PARTS[p]
        at = origin(kid)
        return bufs[arr].at[at[0], at[1], at[2], :, pl.ds(start * unit, size * unit)]

    def forward(arr, p, kid, axis):
        for by in range(1, dims[axis]):
            there = list(kid)
            there[axis] += by
            ref = shard(arr, p, kid)
            copy = pltpu.make_async_remote_copy(
                src_ref=ref, dst_ref=ref,
                send_sem=ag_send.at[sem_id(arr, p, there)],
                recv_sem=ag_recv.at[sem_id(arr, p, there)],
                device_id={"ha": index(moved(me, axis, by))}, device_id_type=MESH,
            )
            copy.start()
            sends[arr].append(copy)

    def arrived(arr, p, kid):
        ref = shard(arr, p, kid)
        pltpu.make_async_remote_copy(
            src_ref=ref, dst_ref=ref,
            send_sem=ag_send.at[sem_id(arr, p, kid)], recv_sem=ag_recv.at[sem_id(arr, p, kid)],
            device_id={"ha": ha}, device_id_type=MESH,
        ).wait_recv()

    every = list(itertools.product(*(range(n) for n in dims)))

    def gather_stage(arr, stage):
        if stage == 0:
            own[arr].wait()
        for p, (_, _, order) in enumerate(GATHER_PARTS):
            for kid in every:
                if stage == 0:
                    take = not any(kid)
                else:
                    take = kid[order[stage - 1]] and not any(kid[a] for a in order[stage:])
                if not take:
                    continue
                if stage:
                    arrived(arr, p, kid)
                for axis in order[stage:]:
                    forward(arr, p, kid, axis)

    depth = min(width, 2048)

    def project(which, lhs, rhs, transposed):
        def block(i):
            cols = pl.ds(pl.multiple_of(i * depth, depth), depth)
            left = lhs[:, :, :, :, cols].reshape(tokens, depth)
            if transposed:
                return contract_cols(left, rhs[:, cols])
            return jnp.dot(left, rhs[cols, :], preferred_element_type=F32)

        part[which] = block(0)

        @pl.loop(1, width // depth)
        def _(i):
            part[which] += block(i)

    wa_copies = []

    def exchange(which):
        for by in range(1, cores):
            copy = pltpu.make_async_remote_copy(
                src_ref=part.at[which], dst_ref=wa_recv.at[by - 1, which],
                send_sem=wa_send.at[by - 1, which], recv_sem=wa_recv_sem.at[by - 1, which],
                device_id={"wa": lax.rem(core + by, cores)}, device_id_type=MESH,
            )
            copy.start()
            wa_copies.append(copy)

    gather_stage(0, 0)
    for load in loads:
        load.start()
    gather_stage(0, 1)
    gather_stage(1, 0)
    gather_stage(0, 2)
    gather_stage(1, 1)
    gather_stage(0, 3)
    x_out = pltpu.make_async_copy(x_buf, xall_ref, copy_sem.at[0])
    x_out.start()
    loads[0].wait()
    project(0, x_buf, wg, False)
    exchange(0)
    gather_stage(1, 2)
    loads[1].wait()
    project(1, x_buf, wu, False)
    exchange(1)
    gather_stage(1, 3)
    g_out = pltpu.make_async_copy(g_buf, gall_ref, copy_sem.at[1])
    g_out.start()
    loads[2].wait()
    project(2, g_buf, wd, True)
    exchange(2)
    x_out.wait()
    for copy in sends[0]:
        copy.wait_send()
    for copy in wa_copies:
        copy.wait()

    slab = 16

    @pl.loop(0, tokens // slab)
    def _(i):
        at = pl.ds(pl.multiple_of(i * slab, slab), slab)
        sums = []
        for which in range(3):
            total = part[which, at, :]
            for by in range(1, cores):
                total = total + wa_recv[by - 1, which, at, :]
            sums.append(total)
        hidden_ref[at, :], gg_ref[at, :], ug_ref[at, :] = pointwise(*sums)

    mine = x_buf
    rs_sends = []

    def spans(p):
        start, size, order = SUM_PARTS[p]
        return start * unit, size * unit, order

    def region(buf, p, order, stage, axis_pos):
        start, size, _ = spans(p)
        at = [slice(None)] * 3
        for a in order[:stage]:
            at[a] = me[a]
        at[order[stage]] = axis_pos
        return buf.at[at[0], at[1], at[2], :, pl.ds(start, size)]

    most = max(dims)

    def sum_send(p, stage):
        _, _, order = spans(p)
        axis = order[stage]
        for by in range(1, dims[axis]):
            there = moved(me, axis, by)
            sem = (p * 3 + stage) * most + by
            copy = pltpu.make_async_remote_copy(
                src_ref=region(mine, p, order, stage, there[axis]),
                dst_ref=region(rs_recv, p, order, stage, me[axis]),
                send_sem=rs_send.at[sem], recv_sem=rs_sem.at[sem],
                device_id={"ha": index(there)}, device_id_type=MESH,
            )
            copy.start()
            rs_sends.append(copy)

    def sum_take(p, stage):
        start, size, order = spans(p)
        axis = order[stage]
        froms = []
        for by in range(1, dims[axis]):
            source = moved(me, axis, -by)
            sem = (p * 3 + stage) * most + by
            ref = region(rs_recv, p, order, stage, source[axis])
            pltpu.make_async_remote_copy(
                src_ref=ref, dst_ref=ref, send_sem=rs_send.at[sem], recv_sem=rs_sem.at[sem],
                device_id={"ha": ha}, device_id_type=MESH,
            ).wait_recv()
            froms.append(source[axis])
        left = [a for a in range(3) if a not in order[: stage + 1]]
        count = 1
        for a in left:
            count *= dims[a]
        cols = pl.ds(start, size)

        def one(i):
            at = [None] * 3
            for a in order[: stage + 1]:
                at[a] = me[a]
            rest = i
            for a in reversed(left):
                at[a] = lax.rem(rest, dims[a])
                rest = lax.div(rest, dims[a])
            total = mine[at[0], at[1], at[2], :, cols].astype(F32)
            for source in froms:
                pos = list(at)
                pos[axis] = source
                total = total + rs_recv[pos[0], pos[1], pos[2], :, cols].astype(F32)
            if left:
                mine[at[0], at[1], at[2], :, cols] = total.astype(BF16)
            else:
                out_ref[:, cols] = total.astype(BF16)

        if left:
            pl.loop(0, count)(one)
        else:
            one(0)

    for p in range(len(SUM_PARTS)):
        start, size, _ = SUM_PARTS[p]

        @pl.loop(start, start + size)
        def _(i):
            cols = pl.ds(pl.multiple_of(i * unit, unit), unit)
            total = contract_cols(gg_ref[...], wg[cols, :]) + contract_cols(ug_ref[...], wu[cols, :])
            mine[:, :, :, :, cols] = total.astype(BF16).reshape(*dims, rows, unit)

        sum_send(p, 0)
    for stage in range(3):
        for p in range(len(SUM_PARTS)):
            sum_take(p, stage)
            if stage < 2:
                sum_send(p, stage + 1)
    for copy in rs_sends + sends[1]:
        copy.wait_send()
    g_out.wait()


def weight_kernel(factor, x_ref, g_ref, hidden_ref, gg_ref, ug_ref, dgate_ref, dup_ref, ddown_ref):
    tokens = hidden_ref.shape[0]
    x = x_ref[...].reshape(tokens, x_ref.shape[-1])
    g = g_ref[...].reshape(tokens, g_ref.shape[-1])
    dgate_ref[...] = (contract_rows(x, gg_ref[...]) * factor).astype(BF16)
    dup_ref[...] = (contract_rows(x, ug_ref[...]) * factor).astype(BF16)
    ddown_ref[...] = (contract_rows(hidden_ref[...], g) * factor).astype(BF16)


def weight_grads(x_all, g_all, hidden, gate_grad, up_grad, factor):
    lead, width = x_all.shape[:-1], x_all.shape[-1]
    tokens, ff = hidden.shape
    step = 512
    gathered = pl.BlockSpec((*lead, step), lambda i: (0, 0, 0, 0, i))
    whole = pl.BlockSpec((tokens, ff), lambda i: (0, 0))
    tall = pl.BlockSpec((step, ff), lambda i: (i, 0))
    return pl.pallas_call(
        functools.partial(weight_kernel, factor),
        grid=(width // step,),
        out_shape=(
            jax.ShapeDtypeStruct((width, ff), BF16),
            jax.ShapeDtypeStruct((width, ff), BF16),
            jax.ShapeDtypeStruct((ff, width), BF16),
        ),
        in_specs=[gathered, gathered, whole, whole, whole],
        out_specs=(tall, tall, pl.BlockSpec((ff, step), lambda i: (0, i))),
        compiler_params=pltpu.CompilerParams(vmem_limit_bytes=VMEM_LIMIT),
        cost_estimate=pl.CostEstimate(
            flops=6 * tokens * ff * width, bytes_accessed=2 * width * (3 * ff + 2 * tokens),
            transcendentals=0,
        ),
    )(x_all, g_all, hidden, gate_grad, up_grad)


def on_device(dims, cores, tokens, cotangent, gate_weight, up_weight, down_weight):
    rows, width = tokens.shape
    ff = gate_weight.shape[1]
    count = rows * dims[0] * dims[1] * dims[2]
    shards = dims[0] * dims[1] * dims[2]
    gathered = (*dims, rows, width)
    hbm = pl.BlockSpec(memory_space=pl.ANY)
    vmem = pl.BlockSpec(memory_space=pltpu.VMEM)
    dma = pltpu.SemaphoreType.DMA
    ag_count = 2 * len(GATHER_PARTS) * shards
    rs_count = 3 * len(SUM_PARTS) * max(dims)
    others = max(cores - 1, 1)
    x_all, g_all, hidden, gate_grad, up_grad, input_grad = pl.pallas_call(
        functools.partial(main_kernel, dims, cores),
        out_shape=(
            jax.ShapeDtypeStruct(gathered, BF16),
            jax.ShapeDtypeStruct(gathered, BF16),
            jax.ShapeDtypeStruct((count, ff), BF16),
            jax.ShapeDtypeStruct((count, ff), BF16),
            jax.ShapeDtypeStruct((count, ff), BF16),
            jax.ShapeDtypeStruct((rows, width), BF16),
        ),
        in_specs=[hbm] * 5,
        out_specs=(hbm, hbm, vmem, vmem, vmem, vmem),
        scratch_shapes=[
            pltpu.VMEM(gathered, BF16),
            pltpu.VMEM(gathered, BF16),
            pltpu.VMEM((width, ff), BF16),
            pltpu.VMEM((width, ff), BF16),
            pltpu.VMEM((ff, width), BF16),
            pltpu.VMEM((3, count, ff), F32),
            pltpu.VMEM((others, 3, count, ff), F32),
            pltpu.VMEM(gathered, BF16),
            dma((2,)), dma((3,)), dma((2,)),
            dma((ag_count,)), dma((ag_count,)),
            dma((others, 3)), dma((others, 3)),
            dma((rs_count,)), dma((rs_count,)),
        ],
        compiler_params=pltpu.CompilerParams(
            collective_id=0, has_side_effects=True, vmem_limit_bytes=VMEM_LIMIT
        ),
        cost_estimate=pl.CostEstimate(
            flops=10 * count * ff * width, bytes_accessed=2 * width * (3 * ff + 2 * count),
            transcendentals=count * ff,
        ),
    )(tokens, cotangent, gate_weight, up_weight, down_weight)
    grads = weight_grads(x_all, g_all, hidden, gate_grad, up_grad, count ** (-0.5))
    return (input_grad, *grads)


def on_device_plain(tokens, cotangent, gate_weight, up_weight, down_weight):
    inputs_all = lax.all_gather(tokens, "ha", axis=0, tiled=True)
    grads_all = lax.all_gather(cotangent, "ha", axis=0, tiled=True)
    factor = inputs_all.shape[0] ** (-0.5)
    gate_part = jnp.dot(inputs_all, gate_weight, preferred_element_type=F32)
    up_part = jnp.dot(inputs_all, up_weight, preferred_element_type=F32)
    hidden_part = contract_cols(grads_all, down_weight)
    gate_sum, up_sum, hidden_grad = lax.psum((gate_part, up_part, hidden_part), "wa")
    hidden, gate_grad, up_grad = pointwise(gate_sum, up_sum, hidden_grad)
    down_weight_grad = (contract_rows(hidden, grads_all) * factor).astype(BF16)
    gate_weight_grad = (contract_rows(inputs_all, gate_grad) * factor).astype(BF16)
    up_weight_grad = (contract_rows(inputs_all, up_grad) * factor).astype(BF16)
    input_grad = lax.psum_scatter(
        contract_cols(gate_grad, gate_weight) + contract_cols(up_grad, up_weight),
        "ha", scatter_dimension=0, tiled=True,
    )
    return (input_grad.astype(BF16), gate_weight_grad, up_weight_grad, down_weight_grad)


def fits(dims, cores, rows, width, ff):
    count = dims[0] * dims[1] * dims[2] * rows
    held = 6 * count * width + 6 * width * ff + 12 * cores * count * ff + 6 * count * ff
    return rows % 16 == 0 and width % 2048 == 0 and ff % 128 == 0 and held < VMEM_LIMIT


def solution(mesh):
    placed = (P("ha", "wa"), P("ha", "wa"), P("wa", "ha"), P("wa", "ha"), P("ha", "wa"))
    cores, along = mesh.shape["wa"], mesh.shape["ha"]
    dims = (along // 4, 2, 2) if along % 4 == 0 else (along, 1, 1)

    def body(tokens, cotangent, gate_weight, up_weight, down_weight):
        plan = on_device_plain
        if fits(dims, cores, *tokens.shape, gate_weight.shape[1]):
            plan = functools.partial(on_device, dims, cores)
        return plan(tokens, cotangent, gate_weight, up_weight, down_weight)

    return jax.shard_map(
        body,
        mesh=mesh,
        in_specs=placed,
        out_specs=(P("ha", "wa"), P("wa", "ha"), P("wa", "ha"), P("ha", "wa")),
        check_vma=False,
    )
```

time: 420 us -> 164 us (0.39)
  waiting for transfers between devices: 281 us -> 0 us
  Pallas kernels: 0 us -> 162 us
  matrix products: 85.2 us -> 0 us
  local copies, waits for them, and re-layouts: 33.4 us -> 0.71 us
  between operations: 13.8 us -> 0.65 us
    pallas_call x0 -> x2, Pallas kernels: none -> 162 us  [the longest x1 141 us: on_device(): pl.pallas_call(functools.partial(main_kernel, dims, cores), out_shape=(ja...]
    all_gather x2 -> x0, waiting for transfers between devices: 140 us -> none  [the longest x1 80.9 us: on_device(): inputs_all = lax.all_gather(tokens, 'ha', axis=0, tiled=True)]
    reduce_scatter x1 -> x0, waiting for transfers between devices: 119 us -> none  [on_device(): lax.psum_scatter(contract_cols(gate_grad, gate_weight) + contract_cols(up...]
    dot_general x8 -> x0, matrix products: 85.2 us -> none  [the longest x3 41 us: contract_cols(): lax.dot_general(left, right, (((1,), (1,)), ((), ())), preferred_element_...]
    unnamed x8 -> x3, local copies, waits for them, and re-layouts: 33.4 us -> 0.71 us
    psum x1 -> x0, waiting for transfers between devices: 20.3 us -> none  [on_device(): lax.psum((gate_part, up_part, hidden_part), 'wa')]
  transfers between devices with their start and end apart: 4 -> 0, of which waited for: 4 -> 0; matrix products, arithmetic and copies ran while one was open for 19% -> 0% of each run, Pallas kernels for 0% -> 0%
where the time goes in v1:
time: 164 us; the launch traced here: 163 us
  Pallas kernels  162 us (99%)
    pallas_call x1, Pallas kernels, on_device(): pl.pallas_call(functools.partial(main_kernel, dims, cores), out_shape=(ja...  141 us
    pallas_call x1, Pallas kernels, weight_grads(): pl.pallas_call(functools.partial(weight_kernel, factor), grid=(width // s...  20.1 us

profile of v1, /device:TPU:0, one launch (start us, length us, event | category | flops | bytes accessed | tf_op | source)
XLA Modules:
  0.0 163.0 jit_solution(5567226459130712765)
XLA Ops:
  0.6 141.5 %shard_map.84 = (bf16[4,2,2,16,8192]{4,3,2,1,0:T(8,128)(2,1)}, bf16[4,2,2,16,8192]{4,3,2,1,0:T(8,128)(2,1)}, bf16[256,768]{1,0:T(8,128)(2,1)}, bf16[256,768]{1,0...) custom-call(bf16[16,8192]{1,0:T(8,128)(2,1)} %tok_ref.1, bf16[16,8192]{1,0:T(8,128)(2,1)} %cot_ref.1, ...), custom_call_target="tpu_custom_call" | custom-call | flops 16106127360 | bytes 46137344 | tf_op jit(solution)/shard_map/pallas_call | solution.py:361
  142.1 0.0 copy-start
  142.1 20.1 %shard_map.85 = (bf16[8192,768]{1,0:T(8,128)(2,1)}, bf16[8192,768]{1,0:T(8,128)(2,1)}, bf16[768,8192]{1,0:T(8,128)(2,1)}) custom-call(bf16[4,2,2,16,8192]{4,3,2,1,0:T(8,128)(2,1)} %get-tuple-element.14.x_ref, bf16[4,2,2,16,8192]{4,3,2,1,0:T(8,128)(2,1)} %get-tuple-element.15.g_ref, bf16[256,768]{1,0:T(8,128)(2,1)} %get-tuple-element.16.hidden_ref, ...), custom_call_target="tpu_custom_call" | custom-call | flops 9663676416 | bytes 46137344 | tf_op jit(solution)/shard_map/pallas_call | solution.py:331
  162.3 0.0 copy-done
  162.3 0.7 copy.10
Async XLA Ops:
  142.1 20.2 %copy-start = (bf16[16,8192]{1,0:T(8,128)(2,1)S(1)}, bf16[16,8192]{1,0:T(8,128)(2,1)}, u32[]{:S(2)}) copy-start(bf16[16,8192]{1,0:T(8,128)(2,1)} %get-tuple-element.26) | copy-start | bytes 786436

commit v2 on v1

--- a/solution.py
+++ b/solution.py
@@ -10,17 +10,22 @@
 
 MESH = pl.DeviceIdType.MESH
 BF16, F32 = jnp.bfloat16, jnp.float32
-VMEM_LIMIT = 60 * 1024 * 1024
-
-GATHER_PARTS = ((0, 7, (0, 1, 2)), (7, 7, (0, 2, 1)), (14, 1, (2, 1, 0)), (15, 1, (1, 2, 0)))
+VMEM_LIMIT = 61 * 1024 * 1024
+
+GATHER_PARTS = ((0, 26, (0, 1, 2)), (26, 26, (0, 2, 1)), (52, 6, (2, 1, 0)), (58, 6, (1, 2, 0)))
 SUM_PARTS = (
-    (0, 4, (2, 1, 0)),
-    (7, 4, (1, 2, 0)),
-    (14, 1, (0, 1, 2)),
-    (15, 1, (0, 2, 1)),
-    (4, 3, (2, 1, 0)),
-    (11, 3, (1, 2, 0)),
+    (0, 4, (0, 1, 2)),
+    (4, 4, (0, 2, 1)),
+    (8, 8, (2, 1, 0)),
+    (16, 8, (1, 2, 0)),
+    (24, 8, (2, 1, 0)),
+    (32, 8, (1, 2, 0)),
+    (40, 8, (2, 1, 0)),
+    (48, 8, (1, 2, 0)),
+    (56, 4, (2, 1, 0)),
+    (60, 4, (1, 2, 0)),
 )
+SUM_WAVES = ((0, 1, 2, 3), (4, 5), (6, 7), (8, 9))
 
 
 def pointwise(gate_sum, up_sum, hidden_grad):
@@ -42,14 +47,14 @@
 def main_kernel(
     dims, cores,
     tok_ref, cot_ref, wg_ref, wu_ref, wd_ref,
-    xall_ref, gall_ref, hidden_ref, gg_ref, ug_ref, out_ref,
-    x_buf, g_buf, wg, wu, wd, part, wa_recv, rs_recv,
+    xt_ref, gall_ref, hidden_t_ref, gg_ref, ug_ref, out_ref,
+    x_buf, g_buf, wg, wu, wd, part, wa_recv, rs_recv, flip, hidden_buf,
     in_sem, w_sem, copy_sem, ag_send, ag_recv, wa_send, wa_recv_sem, rs_send, rs_sem,
 ):
     rows, width = tok_ref.shape
     ff = wg_ref.shape[1]
     tokens = rows * dims[0] * dims[1] * dims[2]
-    unit = width // 16
+    unit = width // 64
     ha = lax.axis_index("ha")
     core = lax.axis_index("wa")
     me = (
@@ -67,7 +72,26 @@
         return (at[0] * dims[1] + at[1]) * dims[2] + at[2]
 
     def origin(kid):
-        return tuple(lax.rem(me[a] - kid[a] + dims[a], dims[a]) for a in range(3))
+        return (
+            me[0] + kid[0],
+            lax.rem(me[1] - kid[1] + dims[1], dims[1]),
+            lax.rem(me[2] - kid[2] + dims[2], dims[2]),
+        )
+
+    def when(conds, run):
+        if not conds:
+            run()
+            return
+        ok = conds[0]()
+        for cond in conds[1:]:
+            ok = jnp.logical_and(ok, cond())
+        pl.when(ok)(run)
+
+    def on_line(by):
+        return lambda: me[0] + by < dims[0] if by > 0 else me[0] + by >= 0
+
+    def exists(kid):
+        return [on_line(kid[0])] if kid[0] else []
 
     barrier = pltpu.get_barrier_semaphore()
     greeted = 0
@@ -96,57 +120,95 @@
     ]
     pl.semaphore_wait(barrier, greeted)
 
-    def sem_id(arr, p, kid):
-        return ((arr * len(GATHER_PARTS) + p) * dims[0] + kid[0]) * dims[1] * dims[2] + (
-            kid[1] * dims[2] + kid[2]
+    shards = dims[0] * dims[1] * dims[2]
+
+    def recv_sem(arr, p, at):
+        return ag_recv.at[(arr * len(GATHER_PARTS) + p) * shards + index(at)]
+
+    sends = {0: [], 1: []}
+    slots = itertools.count()
+
+    def shard(arr, p, at):
+        start, size, _ = GATHER_PARTS[p]
+        return bufs[arr].at[at[0], at[1], at[2], :, pl.ds(start * unit, size * unit)]
+
+    def remote(arr, p, kid, slot, axis, by):
+        at = origin(kid)
+        target = moved(me, axis, by) if by else me
+        ref = shard(arr, p, at)
+        return pltpu.make_async_remote_copy(
+            src_ref=ref, dst_ref=ref, send_sem=ag_send.at[slot], recv_sem=recv_sem(arr, p, at),
+            device_id={"ha": index(target)}, device_id_type=MESH,
         )
 
-    sends = {0: [], 1: []}
-
-    def shard(arr, p, kid):
-        start, size, _ = GATHER_PARTS[p]
-        at = origin(kid)
-        return bufs[arr].at[at[0], at[1], at[2], :, pl.ds(start * unit, size * unit)]
-
     def forward(arr, p, kid, axis):
-        for by in range(1, dims[axis]):
-            there = list(kid)
-            there[axis] += by
-            ref = shard(arr, p, kid)
-            copy = pltpu.make_async_remote_copy(
-                src_ref=ref, dst_ref=ref,
-                send_sem=ag_send.at[sem_id(arr, p, there)],
-                recv_sem=ag_recv.at[sem_id(arr, p, there)],
-                device_id={"ha": index(moved(me, axis, by))}, device_id_type=MESH,
-            )
-            copy.start()
-            sends[arr].append(copy)
-
-    def arrived(arr, p, kid):
-        ref = shard(arr, p, kid)
-        pltpu.make_async_remote_copy(
-            src_ref=ref, dst_ref=ref,
-            send_sem=ag_send.at[sem_id(arr, p, kid)], recv_sem=ag_recv.at[sem_id(arr, p, kid)],
-            device_id={"ha": ha}, device_id_type=MESH,
-        ).wait_recv()
-
-    every = list(itertools.product(*(range(n) for n in dims)))
-
-    def gather_stage(arr, stage):
-        if stage == 0:
-            own[arr].wait()
+        if axis == 0:
+            steps = [1, -1] if kid[0] == 0 else [-1 if kid[0] > 0 else 1]
+        else:
+            steps = range(1, dims[axis])
+        for by in steps:
+            slot = next(slots)
+            conds = []
+            if axis == 0:
+                if dims[0] == 1:
+                    continue
+                conds = [on_line(by)]
+            make = functools.partial(remote, arr, p, kid, slot, axis, by)
+            when(conds, lambda: make().start())
+            sends[arr].append((exists(kid) + conds, make))
+
+    def handle(arr, p, kid):
+        order = GATHER_PARTS[p][2]
+        last = max((order.index(a) for a in range(3) if kid[a]), default=-1)
+
+        def run():
+            if last >= 0:
+                remote(arr, p, kid, 0, 0, 0).wait_recv()
+            for j, axis in enumerate(order):
+                if j > last or (j == last and axis == 0):
+                    forward(arr, p, kid, axis)
+
+        when(exists(kid), run)
+
+    line = [0] + [d for k in range(1, dims[0]) for d in (-k, k)]
+    every = list(itertools.product(line, range(dims[1]), range(dims[2])))
+
+    def kind(p, kid):
+        order = GATHER_PARTS[p][2]
+        last = max((order.index(a) for a in range(3) if kid[a]), default=-1)
+        return last, abs(kid[0])
+
+    def gather(arr, last, dist, line_last=None):
         for p, (_, _, order) in enumerate(GATHER_PARTS):
+            if line_last is not None and line_last != (order[2] == 0):
+                continue
             for kid in every:
-                if stage == 0:
-                    take = not any(kid)
-                else:
-                    take = kid[order[stage - 1]] and not any(kid[a] for a in order[stage:])
-                if not take:
-                    continue
-                if stage:
-                    arrived(arr, p, kid)
-                for axis in order[stage:]:
-                    forward(arr, p, kid, axis)
+                if kind(p, kid) == (last, dist):
+                    handle(arr, p, kid)
+
+    def gather_own(arr):
+        own[arr].wait()
+        gather(arr, -1, 0)
+
+    def gather_begin(arr):
+        gather(arr, 0, 0)
+        gather(arr, 1, 0)
+        for dist in range(1, dims[0]):
+            gather(arr, 0, dist)
+            if dist < dims[0] - 1:
+                gather(arr, 1, dist)
+            if dist > 1:
+                gather(arr, 2, dist - 1, True)
+
+    def gather_rest(arr):
+        if dims[0] > 1:
+            gather(arr, 1, dims[0] - 1)
+
+    def gather_end(arr):
+        for dist in range(dims[0]):
+            gather(arr, 2, dist, False)
+        if dims[0] > 1:
+            gather(arr, 2, dims[0] - 1, True)
 
     depth = min(width, 2048)
 
@@ -176,32 +238,48 @@
             copy.start()
             wa_copies.append(copy)
 
-    gather_stage(0, 0)
+    flips = width // flip.shape[1]
+
+    def flipped(i):
+        return pltpu.make_async_copy(
+            flip.at[i % 2], xt_ref.at[pl.ds(i * flip.shape[1], flip.shape[1]), :],
+            copy_sem.at[i % 2],
+        )
+
+    def transpose_tokens(first, end):
+        for i in range(first, end):
+            if i >= 2:
+                flipped(i - 2).wait()
+            left = x_buf[:, :, :, :, pl.ds(i * flip.shape[1], flip.shape[1])]
+            flip[i % 2] = left.reshape(tokens, flip.shape[1]).T
+            flipped(i).start()
+
+    gather_own(0)
     for load in loads:
         load.start()
-    gather_stage(0, 1)
-    gather_stage(1, 0)
-    gather_stage(0, 2)
-    gather_stage(1, 1)
-    gather_stage(0, 3)
-    x_out = pltpu.make_async_copy(x_buf, xall_ref, copy_sem.at[0])
-    x_out.start()
+    gather_begin(0)
+    gather_own(1)
+    gather_rest(0)
+    gather_begin(1)
+    gather_end(0)
     loads[0].wait()
     project(0, x_buf, wg, False)
     exchange(0)
-    gather_stage(1, 2)
+    gather_rest(1)
     loads[1].wait()
     project(1, x_buf, wu, False)
     exchange(1)
-    gather_stage(1, 3)
-    g_out = pltpu.make_async_copy(g_buf, gall_ref, copy_sem.at[1])
+    transpose_tokens(0, flips)
+    gather_end(1)
+    g_out = pltpu.make_async_copy(g_buf, gall_ref, copy_sem.at[2])
     g_out.start()
     loads[2].wait()
     project(2, g_buf, wd, True)
     exchange(2)
-    x_out.wait()
-    for copy in sends[0]:
-        copy.wait_send()
+    for i in range(max(flips - 2, 0), flips):
+        flipped(i).wait()
+    for conds, make in sends[0]:
+        when(conds, lambda: make().wait_send())
     for copy in wa_copies:
         copy.wait()
 
@@ -216,7 +294,7 @@
             for by in range(1, cores):
                 total = total + wa_recv[by - 1, which, at, :]
             sums.append(total)
-        hidden_ref[at, :], gg_ref[at, :], ug_ref[at, :] = pointwise(*sums)
+        hidden_buf[at, :], gg_ref[at, :], ug_ref[at, :] = pointwise(*sums)
 
     mine = x_buf
     rs_sends = []
@@ -292,40 +370,62 @@
         else:
             one(0)
 
-    for p in range(len(SUM_PARTS)):
+    block = 4 * unit
+
+    def compute(p):
         start, size, _ = SUM_PARTS[p]
 
-        @pl.loop(start, start + size)
+        @pl.loop(start * unit // block, (start + size) * unit // block)
         def _(i):
-            cols = pl.ds(pl.multiple_of(i * unit, unit), unit)
+            cols = pl.ds(pl.multiple_of(i * block, block), block)
             total = contract_cols(gg_ref[...], wg[cols, :]) + contract_cols(ug_ref[...], wu[cols, :])
-            mine[:, :, :, :, cols] = total.astype(BF16).reshape(*dims, rows, unit)
-
-        sum_send(p, 0)
-    for stage in range(3):
-        for p in range(len(SUM_PARTS)):
+            mine[:, :, :, :, cols] = total.astype(BF16).reshape(*dims, rows, block)
+
+    def begin(wave):
+        for p in SUM_WAVES[wave]:
+            compute(p)
+            sum_send(p, 0)
+
+    def advance(wave, stage):
+        for p in SUM_WAVES[wave]:
             sum_take(p, stage)
             if stage < 2:
                 sum_send(p, stage + 1)
-    for copy in rs_sends + sends[1]:
+
+    waves = len(SUM_WAVES)
+    begin(0)
+    begin(1)
+    hidden_t_ref[...] = hidden_buf[...].T
+    for turn in range(waves + 1):
+        if turn < waves:
+            advance(turn, 0)
+        if turn + 2 < waves:
+            begin(turn + 2)
+        if turn >= 1:
+            advance(turn - 1, 1)
+    for wave in range(waves):
+        advance(wave, 2)
+    for copy in rs_sends:
         copy.wait_send()
+    for conds, make in sends[1]:
+        when(conds, lambda: make().wait_send())
     g_out.wait()
 
 
-def weight_kernel(factor, x_ref, g_ref, hidden_ref, gg_ref, ug_ref, dgate_ref, dup_ref, ddown_ref):
-    tokens = hidden_ref.shape[0]
-    x = x_ref[...].reshape(tokens, x_ref.shape[-1])
-    g = g_ref[...].reshape(tokens, g_ref.shape[-1])
-    dgate_ref[...] = (contract_rows(x, gg_ref[...]) * factor).astype(BF16)
-    dup_ref[...] = (contract_rows(x, ug_ref[...]) * factor).astype(BF16)
-    ddown_ref[...] = (contract_rows(hidden_ref[...], g) * factor).astype(BF16)
-
-
-def weight_grads(x_all, g_all, hidden, gate_grad, up_grad, factor):
-    lead, width = x_all.shape[:-1], x_all.shape[-1]
-    tokens, ff = hidden.shape
+def weight_kernel(factor, xt_ref, g_ref, ht_ref, gg_ref, ug_ref, dgate_ref, dup_ref, ddown_ref):
+    def product(left, right):
+        return (jnp.dot(left, right, preferred_element_type=F32) * factor).astype(BF16)
+
+    g = g_ref[...].reshape(ht_ref.shape[1], g_ref.shape[-1])
+    dgate_ref[...] = product(xt_ref[...], gg_ref[...])
+    dup_ref[...] = product(xt_ref[...], ug_ref[...])
+    ddown_ref[...] = product(ht_ref[...], g)
+
+
+def weight_grads(x_t, g_all, hidden_t, gate_grad, up_grad, factor):
+    lead, width = g_all.shape[:-1], g_all.shape[-1]
+    tokens, ff = gate_grad.shape
     step = 512
-    gathered = pl.BlockSpec((*lead, step), lambda i: (0, 0, 0, 0, i))
     whole = pl.BlockSpec((tokens, ff), lambda i: (0, 0))
     tall = pl.BlockSpec((step, ff), lambda i: (i, 0))
     return pl.pallas_call(
@@ -336,14 +436,20 @@
             jax.ShapeDtypeStruct((width, ff), BF16),
             jax.ShapeDtypeStruct((ff, width), BF16),
         ),
-        in_specs=[gathered, gathered, whole, whole, whole],
+        in_specs=[
+            pl.BlockSpec((step, tokens), lambda i: (i, 0)),
+            pl.BlockSpec((*lead, step), lambda i: (0, 0, 0, 0, i)),
+            pl.BlockSpec((ff, tokens), lambda i: (0, 0)),
+            whole,
+            whole,
+        ],
         out_specs=(tall, tall, pl.BlockSpec((ff, step), lambda i: (0, i))),
         compiler_params=pltpu.CompilerParams(vmem_limit_bytes=VMEM_LIMIT),
         cost_estimate=pl.CostEstimate(
             flops=6 * tokens * ff * width, bytes_accessed=2 * width * (3 * ff + 2 * tokens),
             transcendentals=0,
         ),
-    )(x_all, g_all, hidden, gate_grad, up_grad)
+    )(x_t, g_all, hidden_t, gate_grad, up_grad)
 
 
 def on_device(dims, cores, tokens, cotangent, gate_weight, up_weight, down_weight):
@@ -358,12 +464,12 @@
     ag_count = 2 * len(GATHER_PARTS) * shards
     rs_count = 3 * len(SUM_PARTS) * max(dims)
     others = max(cores - 1, 1)
-    x_all, g_all, hidden, gate_grad, up_grad, input_grad = pl.pallas_call(
+    x_t, g_all, hidden_t, gate_grad, up_grad, input_grad = pl.pallas_call(
         functools.partial(main_kernel, dims, cores),
         out_shape=(
+            jax.ShapeDtypeStruct((width, count), BF16),
             jax.ShapeDtypeStruct(gathered, BF16),
-            jax.ShapeDtypeStruct(gathered, BF16),
-            jax.ShapeDtypeStruct((count, ff), BF16),
+            jax.ShapeDtypeStruct((ff, count), BF16),
             jax.ShapeDtypeStruct((count, ff), BF16),
             jax.ShapeDtypeStruct((count, ff), BF16),
             jax.ShapeDtypeStruct((rows, width), BF16),
@@ -379,8 +485,10 @@
             pltpu.VMEM((3, count, ff), F32),
             pltpu.VMEM((others, 3, count, ff), F32),
             pltpu.VMEM(gathered, BF16),
-            dma((2,)), dma((3,)), dma((2,)),
-            dma((ag_count,)), dma((ag_count,)),
+            pltpu.VMEM((2, width // 8, count), BF16),
+            pltpu.VMEM((count, ff), BF16),
+            dma((2,)), dma((3,)), dma((3,)),
+            dma((2 * ag_count,)), dma((ag_count,)),
             dma((others, 3)), dma((others, 3)),
             dma((rs_count,)), dma((rs_count,)),
         ],
@@ -392,7 +500,7 @@
             transcendentals=count * ff,
         ),
     )(tokens, cotangent, gate_weight, up_weight, down_weight)
-    grads = weight_grads(x_all, g_all, hidden, gate_grad, up_grad, count ** (-0.5))
+    grads = weight_grads(x_t, g_all, hidden_t, gate_grad, up_grad, count ** (-0.5))
     return (input_grad, *grads)
 
 

time: 164 us -> 166 us (1.012)
  Pallas kernels: 162 us -> 164 us
    pallas_call x1, Pallas kernels: 141 us -> 145 us  [on_device(): pl.pallas_call(functools.partial(main_kernel, dims, cores), out_shape=(ja...]
where the time goes in v2:
time: 166 us
  Pallas kernels  164 us (99%)
    pallas_call x1, Pallas kernels, on_device(): pl.pallas_call(functools.partial(main_kernel, dims, cores), out_shape=(ja...  145 us
    pallas_call x1, Pallas kernels, weight_grads(): pl.pallas_call(functools.partial(weight_kernel, factor), grid=(width // s...  19.9 us

profile of v2, /device:TPU:0, one launch (start us, length us, event | category | flops | bytes accessed | tf_op | source)
XLA Modules:
  0.0 165.8 jit_solution(17194367244291990557)
XLA Ops:
  0.6 144.5 %shard_map.84 = (bf16[8192,256]{1,0:T(8,128)(2,1)}, bf16[4,2,2,16,8192]{4,3,2,1,0:T(8,128)(2,1)}, bf16[768,256]{1,0:T(8,128)(2,1)}, bf16[256,768]{1,0:T(8,128)(2...) custom-call(bf16[16,8192]{1,0:T(8,128)(2,1)} %tok_ref.1, bf16[16,8192]{1,0:T(8,128)(2,1)} %cot_ref.1, ...), custom_call_target="tpu_custom_call" | custom-call | flops 16106127360 | bytes 46137344 | tf_op jit(solution)/shard_map/pallas_call | solution.py:467
  145.1 0.0 copy-start
  145.2 19.9 %shard_map.85 = (bf16[8192,768]{1,0:T(8,128)(2,1)}, bf16[8192,768]{1,0:T(8,128)(2,1)}, bf16[768,8192]{1,0:T(8,128)(2,1)}) custom-call(bf16[8192,256]{1,0:T(8,128)(2,1)} %get-tuple-element.14.xt_ref, bf16[4,2,2,16,8192]{4,3,2,1,0:T(8,128)(2,1)} %get-tuple-element.15.g_ref, bf16[768,256]{1,0:T(8,128)(2,1)} %get-tuple-element.16.ht_ref, ...), custom_call_target="tpu_custom_call" | custom-call | flops 9663676416 | bytes 46137344 | tf_op jit(solution)/shard_map/pallas_call | solution.py:431
  165.1 0.0 copy-done
  165.1 0.7 copy.10
Async XLA Ops:
  145.1 19.9 %copy-start = (bf16[16,8192]{1,0:T(8,128)(2,1)S(1)}, bf16[16,8192]{1,0:T(8,128)(2,1)}, u32[]{:S(2)}) copy-start(bf16[16,8192]{1,0:T(8,128)(2,1)} %get-tuple-element.26) | copy-start | bytes 786436

commit v3 on v2

--- a/solution.py
+++ b/solution.py
@@ -47,8 +47,8 @@
 def main_kernel(
     dims, cores,
     tok_ref, cot_ref, wg_ref, wu_ref, wd_ref,
-    xt_ref, gall_ref, hidden_t_ref, gg_ref, ug_ref, out_ref,
-    x_buf, g_buf, wg, wu, wd, part, wa_recv, rs_recv, flip, hidden_buf,
+    xall_ref, gall_ref, hidden_ref, gg_ref, ug_ref, out_ref,
+    x_buf, g_buf, wg, wu, wd, part, wa_recv, rs_recv, hid_t, grads_t,
     in_sem, w_sem, copy_sem, ag_send, ag_recv, wa_send, wa_recv_sem, rs_send, rs_sem,
 ):
     rows, width = tok_ref.shape
@@ -212,19 +212,31 @@
 
     depth = min(width, 2048)
 
-    def project(which, lhs, rhs, transposed):
+    def project(which, weight):
         def block(i):
             cols = pl.ds(pl.multiple_of(i * depth, depth), depth)
-            left = lhs[:, :, :, :, cols].reshape(tokens, depth)
-            if transposed:
-                return contract_cols(left, rhs[:, cols])
-            return jnp.dot(left, rhs[cols, :], preferred_element_type=F32)
+            left = x_buf[:, :, :, :, cols].reshape(tokens, depth)
+            return jnp.dot(left, weight[cols, :], preferred_element_type=F32)
 
         part[which] = block(0)
 
         @pl.loop(1, width // depth)
         def _(i):
             part[which] += block(i)
+
+    def project_hidden():
+        def block(i):
+            cols = pl.ds(pl.multiple_of(i * depth, depth), depth)
+            right = g_buf[:, :, :, :, cols].reshape(tokens, depth)
+            return contract_cols(wd[:, cols], right)
+
+        hid_t[...] = block(0)
+
+        @pl.loop(1, width // depth)
+        def _(i):
+            hid_t[...] += block(i)
+
+        part[2] = hid_t[...].T
 
     wa_copies = []
 
@@ -238,22 +250,6 @@
             copy.start()
             wa_copies.append(copy)
 
-    flips = width // flip.shape[1]
-
-    def flipped(i):
-        return pltpu.make_async_copy(
-            flip.at[i % 2], xt_ref.at[pl.ds(i * flip.shape[1], flip.shape[1]), :],
-            copy_sem.at[i % 2],
-        )
-
-    def transpose_tokens(first, end):
-        for i in range(first, end):
-            if i >= 2:
-                flipped(i - 2).wait()
-            left = x_buf[:, :, :, :, pl.ds(i * flip.shape[1], flip.shape[1])]
-            flip[i % 2] = left.reshape(tokens, flip.shape[1]).T
-            flipped(i).start()
-
     gather_own(0)
     for load in loads:
         load.start()
@@ -262,22 +258,22 @@
     gather_rest(0)
     gather_begin(1)
     gather_end(0)
+    x_out = pltpu.make_async_copy(x_buf, xall_ref, copy_sem.at[0])
+    x_out.start()
     loads[0].wait()
-    project(0, x_buf, wg, False)
+    project(0, wg)
     exchange(0)
     gather_rest(1)
     loads[1].wait()
-    project(1, x_buf, wu, False)
+    project(1, wu)
     exchange(1)
-    transpose_tokens(0, flips)
     gather_end(1)
-    g_out = pltpu.make_async_copy(g_buf, gall_ref, copy_sem.at[2])
+    g_out = pltpu.make_async_copy(g_buf, gall_ref, copy_sem.at[1])
     g_out.start()
     loads[2].wait()
-    project(2, g_buf, wd, True)
+    project_hidden()
     exchange(2)
-    for i in range(max(flips - 2, 0), flips):
-        flipped(i).wait()
+    x_out.wait()
     for conds, make in sends[0]:
         when(conds, lambda: make().wait_send())
     for copy in wa_copies:
@@ -294,7 +290,10 @@
             for by in range(1, cores):
                 total = total + wa_recv[by - 1, which, at, :]
             sums.append(total)
-        hidden_buf[at, :], gg_ref[at, :], ug_ref[at, :] = pointwise(*sums)
+        hidden_ref[at, :], gg_ref[at, :], ug_ref[at, :] = pointwise(*sums)
+
+    grads_t[0] = gg_ref[...].T
+    grads_t[1] = ug_ref[...].T
 
     mine = x_buf
     rs_sends = []
@@ -378,8 +377,9 @@
         @pl.loop(start * unit // block, (start + size) * unit // block)
         def _(i):
             cols = pl.ds(pl.multiple_of(i * block, block), block)
-            total = contract_cols(gg_ref[...], wg[cols, :]) + contract_cols(ug_ref[...], wu[cols, :])
-            mine[:, :, :, :, cols] = total.astype(BF16).reshape(*dims, rows, block)
+            total = jnp.dot(wg[cols, :], grads_t[0], preferred_element_type=F32)
+            total = total + jnp.dot(wu[cols, :], grads_t[1], preferred_element_type=F32)
+            mine[:, :, :, :, cols] = total.astype(BF16).T.reshape(*dims, rows, block)
 
     def begin(wave):
         for p in SUM_WAVES[wave]:
@@ -395,7 +395,6 @@
     waves = len(SUM_WAVES)
     begin(0)
     begin(1)
-    hidden_t_ref[...] = hidden_buf[...].T
     for turn in range(waves + 1):
         if turn < waves:
             advance(turn, 0)
@@ -412,20 +411,20 @@
     g_out.wait()
 
 
-def weight_kernel(factor, xt_ref, g_ref, ht_ref, gg_ref, ug_ref, dgate_ref, dup_ref, ddown_ref):
-    def product(left, right):
-        return (jnp.dot(left, right, preferred_element_type=F32) * factor).astype(BF16)
-
-    g = g_ref[...].reshape(ht_ref.shape[1], g_ref.shape[-1])
-    dgate_ref[...] = product(xt_ref[...], gg_ref[...])
-    dup_ref[...] = product(xt_ref[...], ug_ref[...])
-    ddown_ref[...] = product(ht_ref[...], g)
-
-
-def weight_grads(x_t, g_all, hidden_t, gate_grad, up_grad, factor):
-    lead, width = g_all.shape[:-1], g_all.shape[-1]
-    tokens, ff = gate_grad.shape
+def weight_kernel(factor, x_ref, g_ref, hidden_ref, gg_ref, ug_ref, dgate_ref, dup_ref, ddown_ref):
+    tokens = hidden_ref.shape[0]
+    x = x_ref[...].reshape(tokens, x_ref.shape[-1])
+    g = g_ref[...].reshape(tokens, g_ref.shape[-1])
+    dgate_ref[...] = (contract_rows(x, gg_ref[...]) * factor).astype(BF16)
+    dup_ref[...] = (contract_rows(x, ug_ref[...]) * factor).astype(BF16)
+    ddown_ref[...] = (contract_rows(hidden_ref[...], g) * factor).astype(BF16)
+
+
+def weight_grads(x_all, g_all, hidden, gate_grad, up_grad, factor):
+    lead, width = x_all.shape[:-1], x_all.shape[-1]
+    tokens, ff = hidden.shape
     step = 512
+    gathered = pl.BlockSpec((*lead, step), lambda i: (0, 0, 0, 0, i))
     whole = pl.BlockSpec((tokens, ff), lambda i: (0, 0))
     tall = pl.BlockSpec((step, ff), lambda i: (i, 0))
     return pl.pallas_call(
@@ -436,20 +435,14 @@
             jax.ShapeDtypeStruct((width, ff), BF16),
             jax.ShapeDtypeStruct((ff, width), BF16),
         ),
-        in_specs=[
-            pl.BlockSpec((step, tokens), lambda i: (i, 0)),
-            pl.BlockSpec((*lead, step), lambda i: (0, 0, 0, 0, i)),
-            pl.BlockSpec((ff, tokens), lambda i: (0, 0)),
-            whole,
-            whole,
-        ],
+        in_specs=[gathered, gathered, whole, whole, whole],
         out_specs=(tall, tall, pl.BlockSpec((ff, step), lambda i: (0, i))),
         compiler_params=pltpu.CompilerParams(vmem_limit_bytes=VMEM_LIMIT),
         cost_estimate=pl.CostEstimate(
             flops=6 * tokens * ff * width, bytes_accessed=2 * width * (3 * ff + 2 * tokens),
             transcendentals=0,
         ),
-    )(x_t, g_all, hidden_t, gate_grad, up_grad)
+    )(x_all, g_all, hidden, gate_grad, up_grad)
 
 
 def on_device(dims, cores, tokens, cotangent, gate_weight, up_weight, down_weight):
@@ -464,12 +457,12 @@
     ag_count = 2 * len(GATHER_PARTS) * shards
     rs_count = 3 * len(SUM_PARTS) * max(dims)
     others = max(cores - 1, 1)
-    x_t, g_all, hidden_t, gate_grad, up_grad, input_grad = pl.pallas_call(
+    x_all, g_all, hidden, gate_grad, up_grad, input_grad = pl.pallas_call(
         functools.partial(main_kernel, dims, cores),
         out_shape=(
-            jax.ShapeDtypeStruct((width, count), BF16),
             jax.ShapeDtypeStruct(gathered, BF16),
-            jax.ShapeDtypeStruct((ff, count), BF16),
+            jax.ShapeDtypeStruct(gathered, BF16),
+            jax.ShapeDtypeStruct((count, ff), BF16),
             jax.ShapeDtypeStruct((count, ff), BF16),
             jax.ShapeDtypeStruct((count, ff), BF16),
             jax.ShapeDtypeStruct((rows, width), BF16),
@@ -485,9 +478,9 @@
             pltpu.VMEM((3, count, ff), F32),
             pltpu.VMEM((others, 3, count, ff), F32),
             pltpu.VMEM(gathered, BF16),
-            pltpu.VMEM((2, width // 8, count), BF16),
-            pltpu.VMEM((count, ff), BF16),
-            dma((2,)), dma((3,)), dma((3,)),
+            pltpu.VMEM((ff, count), F32),
+            pltpu.VMEM((2, ff, count), BF16),
+            dma((2,)), dma((3,)), dma((2,)),
             dma((2 * ag_count,)), dma((ag_count,)),
             dma((others, 3)), dma((others, 3)),
             dma((rs_count,)), dma((rs_count,)),
@@ -500,7 +493,7 @@
             transcendentals=count * ff,
         ),
     )(tokens, cotangent, gate_weight, up_weight, down_weight)
-    grads = weight_grads(x_t, g_all, hidden_t, gate_grad, up_grad, count ** (-0.5))
+    grads = weight_grads(x_all, g_all, hidden, gate_grad, up_grad, count ** (-0.5))
     return (input_grad, *grads)
 
 

time: 166 us -> 164 us (0.988)
    pallas_call x1, Pallas kernels: 145 us -> 142 us  [on_device(): pl.pallas_call(functools.partial(main_kernel, dims, cores), out_shape=(ja...]
where the time goes in v3:
time: 164 us
  Pallas kernels  163 us (99%)
    pallas_call x1, Pallas kernels, on_device(): pl.pallas_call(functools.partial(main_kernel, dims, cores), out_shape=(ja...  142 us
    pallas_call x1, Pallas kernels, weight_grads(): pl.pallas_call(functools.partial(weight_kernel, factor), grid=(width // s...  20.1 us

profile of v3, /device:TPU:0, one launch (start us, length us, event | category | flops | bytes accessed | tf_op | source)
XLA Modules:
  0.0 163.9 jit_solution(11055736994135334912)
XLA Ops:
  0.6 142.4 %shard_map.84 = (bf16[4,2,2,16,8192]{4,3,2,1,0:T(8,128)(2,1)}, bf16[4,2,2,16,8192]{4,3,2,1,0:T(8,128)(2,1)}, bf16[256,768]{1,0:T(8,128)(2,1)}, bf16[256,768]{1,0...) custom-call(bf16[16,8192]{1,0:T(8,128)(2,1)} %tok_ref.1, bf16[16,8192]{1,0:T(8,128)(2,1)} %cot_ref.1, ...), custom_call_target="tpu_custom_call" | custom-call | flops 16106127360 | bytes 46137344 | tf_op jit(solution)/shard_map/pallas_call | solution.py:460
  143.0 0.0 copy-start
  143.0 20.1 %shard_map.85 = (bf16[8192,768]{1,0:T(8,128)(2,1)}, bf16[8192,768]{1,0:T(8,128)(2,1)}, bf16[768,8192]{1,0:T(8,128)(2,1)}) custom-call(bf16[4,2,2,16,8192]{4,3,2,1,0:T(8,128)(2,1)} %get-tuple-element.14.x_ref, bf16[4,2,2,16,8192]{4,3,2,1,0:T(8,128)(2,1)} %get-tuple-element.15.g_ref, bf16[256,768]{1,0:T(8,128)(2,1)} %get-tuple-element.16.hidden_ref, ...), custom_call_target="tpu_custom_call" | custom-call | flops 9663676416 | bytes 46137344 | tf_op jit(solution)/shard_map/pallas_call | solution.py:430
  163.2 0.0 copy-done
  163.2 0.7 copy.10
Async XLA Ops:
  143.0 20.2 %copy-start = (bf16[16,8192]{1,0:T(8,128)(2,1)S(1)}, bf16[16,8192]{1,0:T(8,128)(2,1)}, u32[]{:S(2)}) copy-start(bf16[16,8192]{1,0:T(8,128)(2,1)} %get-tuple-element.26) | copy-start | bytes 786436

commit v4 on v1

--- a/solution.py
+++ b/solution.py
@@ -10,7 +10,7 @@
 
 MESH = pl.DeviceIdType.MESH
 BF16, F32 = jnp.bfloat16, jnp.float32
-VMEM_LIMIT = 60 * 1024 * 1024
+VMEM_LIMIT = 61 * 1024 * 1024
 
 GATHER_PARTS = ((0, 7, (0, 1, 2)), (7, 7, (0, 2, 1)), (14, 1, (2, 1, 0)), (15, 1, (1, 2, 0)))
 SUM_PARTS = (
@@ -43,7 +43,7 @@
     dims, cores,
     tok_ref, cot_ref, wg_ref, wu_ref, wd_ref,
     xall_ref, gall_ref, hidden_ref, gg_ref, ug_ref, out_ref,
-    x_buf, g_buf, wg, wu, wd, part, wa_recv, rs_recv,
+    x_buf, g_buf, wg, wu, wd, part, wa_recv, rs_recv, hid_t, grads_t,
     in_sem, w_sem, copy_sem, ag_send, ag_recv, wa_send, wa_recv_sem, rs_send, rs_sem,
 ):
     rows, width = tok_ref.shape
@@ -150,19 +150,31 @@
 
     depth = min(width, 2048)
 
-    def project(which, lhs, rhs, transposed):
+    def project(which, weight):
         def block(i):
             cols = pl.ds(pl.multiple_of(i * depth, depth), depth)
-            left = lhs[:, :, :, :, cols].reshape(tokens, depth)
-            if transposed:
-                return contract_cols(left, rhs[:, cols])
-            return jnp.dot(left, rhs[cols, :], preferred_element_type=F32)
+            left = x_buf[:, :, :, :, cols].reshape(tokens, depth)
+            return jnp.dot(left, weight[cols, :], preferred_element_type=F32)
 
         part[which] = block(0)
 
         @pl.loop(1, width // depth)
         def _(i):
             part[which] += block(i)
+
+    def project_hidden():
+        def block(i):
+            cols = pl.ds(pl.multiple_of(i * depth, depth), depth)
+            right = g_buf[:, :, :, :, cols].reshape(tokens, depth)
+            return contract_cols(wd[:, cols], right)
+
+        hid_t[...] = block(0)
+
+        @pl.loop(1, width // depth)
+        def _(i):
+            hid_t[...] += block(i)
+
+        part[2] = hid_t[...].T
 
     wa_copies = []
 
@@ -187,17 +199,17 @@
     x_out = pltpu.make_async_copy(x_buf, xall_ref, copy_sem.at[0])
     x_out.start()
     loads[0].wait()
-    project(0, x_buf, wg, False)
+    project(0, wg)
     exchange(0)
     gather_stage(1, 2)
     loads[1].wait()
-    project(1, x_buf, wu, False)
+    project(1, wu)
     exchange(1)
     gather_stage(1, 3)
     g_out = pltpu.make_async_copy(g_buf, gall_ref, copy_sem.at[1])
     g_out.start()
     loads[2].wait()
-    project(2, g_buf, wd, True)
+    project_hidden()
     exchange(2)
     x_out.wait()
     for copy in sends[0]:
@@ -217,6 +229,9 @@
                 total = total + wa_recv[by - 1, which, at, :]
             sums.append(total)
         hidden_ref[at, :], gg_ref[at, :], ug_ref[at, :] = pointwise(*sums)
+
+    grads_t[0] = gg_ref[...].T
+    grads_t[1] = ug_ref[...].T
 
     mine = x_buf
     rs_sends = []
@@ -298,8 +313,9 @@
         @pl.loop(start, start + size)
         def _(i):
             cols = pl.ds(pl.multiple_of(i * unit, unit), unit)
-            total = contract_cols(gg_ref[...], wg[cols, :]) + contract_cols(ug_ref[...], wu[cols, :])
-            mine[:, :, :, :, cols] = total.astype(BF16).reshape(*dims, rows, unit)
+            total = jnp.dot(wg[cols, :], grads_t[0], preferred_element_type=F32)
+            total = total + jnp.dot(wu[cols, :], grads_t[1], preferred_element_type=F32)
+            mine[:, :, :, :, cols] = total.astype(BF16).T.reshape(*dims, rows, unit)
 
         sum_send(p, 0)
     for stage in range(3):
@@ -379,6 +395,8 @@
             pltpu.VMEM((3, count, ff), F32),
             pltpu.VMEM((others, 3, count, ff), F32),
             pltpu.VMEM(gathered, BF16),
+            pltpu.VMEM((ff, count), F32),
+            pltpu.VMEM((2, ff, count), BF16),
             dma((2,)), dma((3,)), dma((2,)),
             dma((ag_count,)), dma((ag_count,)),
             dma((others, 3)), dma((others, 3)),

time: 164 us -> 164 us (level)
  no operation moved by 1% of the time
where the time goes in v4:
time: 164 us
  Pallas kernels  162 us (99%)
    pallas_call x1, Pallas kernels, on_device(): pl.pallas_call(functools.partial(main_kernel, dims, cores), out_shape=(ja...  142 us
    pallas_call x1, Pallas kernels, weight_grads(): pl.pallas_call(functools.partial(weight_kernel, factor), grid=(width // s...  20.1 us

profile of v4, /device:TPU:0, one launch (start us, length us, event | category | flops | bytes accessed | tf_op | source)
XLA Modules:
  0.0 163.7 jit_solution(6977098290001982619)
XLA Ops:
  0.6 142.2 %shard_map.84 = (bf16[4,2,2,16,8192]{4,3,2,1,0:T(8,128)(2,1)}, bf16[4,2,2,16,8192]{4,3,2,1,0:T(8,128)(2,1)}, bf16[256,768]{1,0:T(8,128)(2,1)}, bf16[256,768]{1,0...) custom-call(bf16[16,8192]{1,0:T(8,128)(2,1)} %tok_ref.1, bf16[16,8192]{1,0:T(8,128)(2,1)} %cot_ref.1, ...), custom_call_target="tpu_custom_call" | custom-call | flops 16106127360 | bytes 46137344 | tf_op jit(solution)/shard_map/pallas_call | solution.py:377
  142.8 0.0 copy-start
  142.9 20.1 %shard_map.85 = (bf16[8192,768]{1,0:T(8,128)(2,1)}, bf16[8192,768]{1,0:T(8,128)(2,1)}, bf16[768,8192]{1,0:T(8,128)(2,1)}) custom-call(bf16[4,2,2,16,8192]{4,3,2,1,0:T(8,128)(2,1)} %get-tuple-element.14.x_ref, bf16[4,2,2,16,8192]{4,3,2,1,0:T(8,128)(2,1)} %get-tuple-element.15.g_ref, bf16[256,768]{1,0:T(8,128)(2,1)} %get-tuple-element.16.hidden_ref, ...), custom_call_target="tpu_custom_call" | custom-call | flops 9663676416 | bytes 46137344 | tf_op jit(solution)/shard_map/pallas_call | solution.py:347
  163.0 0.0 copy-done
  163.0 0.7 copy.10
Async XLA Ops:
  142.8 20.2 %copy-start = (bf16[16,8192]{1,0:T(8,128)(2,1)S(1)}, bf16[16,8192]{1,0:T(8,128)(2,1)}, u32[]{:S(2)}) copy-start(bf16[16,8192]{1,0:T(8,128)(2,1)} %get-tuple-element.26) | copy-start | bytes 786436
